TPU v7x, 32 devices: a whole 2x2x4 slice. The times are simulated.
32 devices in a mesh: wind: 2 (over y), gx: 4 (over z), gy: 2 (over x), gz: 2 (over core).
Axes of the slice: x: 2, y: 2, z: 4, core: 2. Of those that a mesh axis runs over, the one named last changes fastest.
Arguments:
- pressure: bfloat16 [8192, 8192], P(('wind', 'gx'), ('gy', 'gz')), parts along dimension 0, may hold values from -40 to 40
- fir_taps: bfloat16 [257], replicated, may hold values from -0.375 to 0.375
- influence: bfloat16 [256, 4, 4, 512], P(None, ('gy', 'gz'), 'gx'), may hold values from -0.0625 to 0.0625
- mode_impulse: float32 [256, 64], replicated, may hold values from -0.75 to 0.75
- mode_taps: int32 [256], replicated, may hold values from 1 to 64, as said below
Outputs:
- responses: bfloat16 [512, 4096], P(('wind', 'gx', 'gy', 'gz')), parts along dimension 0
- correlation_score: float32 [512, 4, 4, 512], P('wind', ('gy', 'gz'), 'gx'), parts along dimension 0
There are 2 independent parts, one for each index of `wind`. A program takes and returns all parts, laid end to end along the dimension named above; an argument that names none is the same for every part. Nothing has to cross between parts.
Inputs may be any that keep to these rules, and one draw needn't show every extreme that they name: `mode_taps`: some mode keeps all 64 taps.
All inputs are finite; a program needn't handle non-finite values.
Results may differ from a plain program's by a relative error of at most 0.005.
Values may be sent and summed in bfloat16 or wider, within the bound.
A program may use at most 64 MiB of HBM per device.

v0:
```python
import math
import jax
import jax.numpy as jnp
from jax import lax
from jax.sharding import PartitionSpec as P

F32 = jnp.float32
BF16 = jnp.bfloat16


def dot(a, b, contract):
    return lax.dot_general(a, b, (contract, ((), ())), preferred_element_type=F32)


def band_matrix(tap_row, row_count):
    tap_count = tap_row.shape[0]
    extended = jnp.concatenate([tap_row, jnp.zeros((row_count,), tap_row.dtype)])
    flat = jnp.tile(extended, row_count)[: row_count * (row_count + tap_count - 1)]
    return flat.reshape(row_count, row_count + tap_count - 1)


def windows(padded, block, width):
    count = (padded.shape[1] - (width - block)) // block
    return jnp.stack([padded[:, i * block : i * block + width] for i in range(count)], axis=1)


def dynamic_filter(series, impulse, tap_limits):
    impulse_len = impulse.shape[1]
    kept_mask = jnp.arange(impulse_len, dtype=jnp.int32)[None, :] < tap_limits[:, None]
    kernel_taps = jnp.where(kept_mask, impulse, jnp.zeros_like(impulse))[:, ::-1]
    result = lax.conv_general_dilated(
        series[None],
        kernel_taps[:, None, :],
        window_strides=(1,),
        padding=[(impulse_len - 1, 0)],
        dimension_numbers=("NCH", "OIH", "NCH"),
        feature_group_count=series.shape[0],
        precision=lax.Precision.HIGHEST,
    )
    return result[0]


def panel_moments(pressure, halo, band, block):
    rows = pressure.shape[0]
    padded = jnp.concatenate([halo, pressure], axis=0)
    width = band.shape[1]
    parts = [dot(band, padded[o : o + width], ((1,), (0,))) for o in range(0, rows, block)]
    filtered = jnp.concatenate(parts, axis=0).astype(BF16)
    wide = filtered.astype(F32)
    mean = jnp.mean(wide, axis=0)
    spread = jnp.sum(jnp.square(wide - mean[None, :]), axis=0)
    return (mean, spread)


def body(pressure, fir_taps, influence, mode_impulse, mode_taps):
    nx, ng = (lax.axis_size("gx"), lax.axis_size(("gy", "gz")))
    rows, panels = pressure.shape
    total = rows * nx
    rim = fir_taps.shape[0] - 1
    modes = influence.shape[0]
    own = modes // (nx * ng)
    own_panels = panels // nx
    block = min(512, rows)
    lines = lax.all_gather(influence.reshape(modes, -1), "gx", axis=1, tiled=True)
    halo = lax.ppermute(pressure[rows - rim :], "gx", [(i, i + 1) for i in range(nx - 1)])
    raw = dot(lines, pressure, ((1,), (1,)))
    raw = lax.psum_scatter(
        raw.reshape(nx, ng * own, rows), ("gy", "gz"), scatter_dimension=1, tiled=True
    )
    raw = lax.all_to_all(raw, "gx", split_axis=0, concat_axis=0, tiled=True)
    raw = raw.transpose(1, 0, 2).reshape(own, total)
    forward = band_matrix(fir_taps, 512)
    backward = band_matrix(fir_taps[::-1], 512)
    width = forward.shape[1]
    padded = jnp.pad(raw, ((0, 0), (rim, 0)))
    high = padded.astype(BF16)
    low = (padded - high.astype(F32)).astype(BF16)
    loads = sum(
        (
            dot(windows(x, 512, width).reshape(-1, width), backward, ((1,), (1,)))
            for x in (high, low)
        )
    ).reshape(own, total)
    first_mode = lax.axis_index(("gx", "gy", "gz")) * own
    own_impulse = lax.dynamic_slice_in_dim(mode_impulse, first_mode, own, 0)
    own_limits = lax.dynamic_slice_in_dim(mode_taps, first_mode, own, 0)
    responses = dynamic_filter(loads, own_impulse, own_limits).astype(BF16)
    resp_wide = responses.astype(F32)
    mean_mode = jnp.mean(resp_wide, axis=1)
    spread_mode = jnp.sqrt(jnp.mean(jnp.square(resp_wide - mean_mode[:, None]), axis=1) + 1e-06)
    ahead = windows(jnp.pad(responses, ((0, 0), (0, rim))), 512, width).reshape(-1, width)
    back = dot(ahead, forward, ((1,), (1,))).reshape(own, total)
    left = total - 1 - jnp.arange(total, dtype=jnp.int32)
    within = jnp.arange(rim + 1, dtype=jnp.int32)[:, None] <= left[None, :]
    reach = jnp.sum(jnp.where(within, fir_taps.astype(F32)[:, None], 0.0), axis=0)
    scale = 1.0 / (math.sqrt(total) * spread_mode)
    back = ((back - mean_mode[:, None] * reach[None, :]) * scale[:, None]).astype(BF16)
    back = back.reshape(own, nx, rows).transpose(1, 0, 2)
    back = lax.all_to_all(back, "gx", split_axis=0, concat_axis=0, tiled=True)
    back = lax.all_gather(back, ("gy", "gz"), axis=1, tiled=True).reshape(modes, rows)
    cross = dot(back, pressure, ((1,), (0,))).astype(BF16)
    cross = lax.all_to_all(
        cross.reshape(modes, nx, own_panels), "gx", split_axis=1, concat_axis=1, tiled=True
    )
    cross = jnp.sum(cross.astype(F32), axis=1)
    mean_part, square_part = panel_moments(
        pressure, halo, band_matrix(fir_taps[::-1], block), block
    )
    moments = jnp.stack([mean_part, square_part]).reshape(2, nx, own_panels)
    moments = lax.all_to_all(moments, "gx", split_axis=1, concat_axis=1, tiled=True)
    mean_panel = jnp.mean(moments[0], axis=0)
    squares = jnp.sum(moments[1] + rows * jnp.square(moments[0] - mean_panel[None, :]), axis=0)
    spread_panel = jnp.sqrt(squares / total + 1e-06)
    scores = cross / spread_panel[None, :]
    return (responses, scores.reshape(influence.shape))


def solution(mesh):
    return jax.shard_map(
        body,
        mesh=mesh,
        in_specs=(
            P(("wind", "gx"), ("gy", "gz")),
            P(),
            P(None, ("gy", "gz"), "gx", None),
            P(),
            P(),
        ),
        out_specs=(P(("wind", "gx", "gy", "gz"), None), P("wind", ("gy", "gz"), "gx", None)),
        check_vma=False,
    )
```

profile of v0, /device:TPU:0, one launch (start us, length us, event | category | flops | bytes accessed | tf_op | source)
XLA Modules:
  0.0 195.6 jit_solution(10294810391997105271)
XLA Ops:
  7.2 0.7 all-gather.3.cloned.1.call-update
  8.0 2.3 %slice.128 = bf16[256,2048]{1,0:T(8,128)(2,1)} slice(bf16[1024,2048]{1,0:T(8,128)(2,1)} %param.5), slice={[768:1024], [0:2048]} | slice | bytes 2097152 | tf_op jit(solution)/shard_map/slice | solution.py:65
  10.3 5.9 %collective-permute-start = (bf16[256,2048]{1,0:T(8,128)(2,1)}, bf16[256,2048]{1,0:T(8,128)(2,1)}, u32[]{:S(2)}, u32[]{:S(2)}) collective-permute-start(bf16[256,2048]{1,0:T(8,128)(2,1)} %slice.128), channel_id=1, source_target_pairs={{0,4},{4,8},{8,12},{1,5},{5,9},{9,13},{2,6},{6,10},{10,14},{3,7},{... | collective-permute-start | bytes 3145736 | tf_op jit(solution)/shard_map/ppermute | solution.py:65
  16.2 0.7 convert_element_type.45
  16.9 0.8 reverse
  17.7 0.7 concatenate.16
  18.5 1.3 tile.9
  19.9 0.7 reshape.132
  20.9 1.3 tile.11
  22.3 1.6 reshape.135
  23.8 3.7 %fusion.7 = bf16[512,2048]{1,0:T(8,128)(2,1)S(1)} fusion(bf16[512,768]{1,0:T(8,128)(2,1)S(1)} %reshape.132, bf16[1024,2048]{1,0:T(8,128)(2,1)} %param.5), kind=kOutput, calls=%fused_computation.13 | convolution fusion | flops 1611661312 | bytes 6029312 | tf_op jit(solution)/shard_map/dot_general | solution.py:12
  27.5 26.4 %all-gather.3.cloned.1.call-done = bf16[256,1,1,2048]{3,0,2,1:T(8,128)(2,1)} async-done(((bf16[256,1,1,512]{3,0,2,1:T(8,128)(2,1)}), bf16[256,1,1,2048]{3,0,2,1:T(8,128)(2,1)}) %all-gather.3.cloned.1.call-update) | async-done | bytes 1048592 | tf_op jit(solution)/shard_map/all_gather | solution.py:64
  54.0 3.8 %fusion.17 = f32[256,1024]{1,0:T(8,128)S(1)} fusion(bf16[1024,2048]{1,0:T(8,128)(2,1)} %param.5, bf16[256,1,1,2048]{3,0,2,1:T(8,128)(2,1)} %all-gather.3.cloned.1.call-done), kind=kOutput, calls=%fused_computation.26 | convolution fusion | flops 1073741824 | bytes 6291456 | tf_op jit(solution)/shard_map/dot_general | solution.py:12
  57.8 1.7 copy.44
  59.5 0.8 select_reduce_fusion
  60.3 0.6 dynamic-slice
  61.5 5.0 %fusion.6 = bf16[512,2048]{1,0:T(8,128)(2,1)} fusion(bf16[512,768]{1,0:T(8,128)(2,1)S(1)} %reshape.132, bf16[1024,2048]{1,0:T(8,128)(2,1)} %param.5, bf16[256,2048]{1,0:T(8,128)(2,1)} %collective-permute-done), kind=kOutput, calls=%fused_computation.12 | convolution fusion | flops 1617952768 | bytes 8126464 | tf_op jit(solution)/shard_map/dot_general | solution.py:12
  66.5 29.7 %all-reduce.7.cloned.1.call-done = f32[4,64,1024]{2,0,1:T(4,128)} async-done(((f32[4,64,1024]{2,0,1:T(4,128)}), f32[4,64,1024]{2,0,1:T(4,128)}) %all-reduce.7.cloned.1.call-update) | async-done | bytes 1048592
  96.2 1.0 constant_dynamic-slice_fusion
  97.2 0.9 copy.45
  98.0 4.6 %all-to-all-start = ((f32[4,16,1024]{2,1,0:T(8,128)}), f32[4,16,1024]{2,1,0:T(8,128)S(1)}, u32[]{:S(2)}, u32[]{:S(2)}) async-start(f32[4,16,1024]{2,1,0:T(8,128)} %copy.45), calls=%async_computation | async-start | bytes 524288 | tf_op jit(solution)/shard_map/all_to_all | solution.py:70
  102.6 2.2 %convert_reduce_fusion = f32[2048]{0:T(1024)S(1)} fusion(bf16[512,2048]{1,0:T(8,128)(2,1)S(1)} %fusion.7, bf16[512,2048]{1,0:T(8,128)(2,1)} %fusion.6), kind=kLoop, calls=%fused_computation.1 | loop fusion | flops 10483712 | bytes 4202496 | tf_op jit(solution)/shard_map/reduce_sum | solution.py:50
  104.9 6.2 %all-to-all-done = f32[4,16,1024]{2,1,0:T(8,128)S(1)} async-done(((f32[4,16,1024]{2,1,0:T(8,128)}), f32[4,16,1024]{2,1,0:T(8,128)S(1)}, u32[]{:S(2)}, u32[]{:S(2)}) %all-to-all-start) | async-done | bytes 262176 | tf_op jit(solution)/shard_map/all_to_all | solution.py:70
  111.2 0.4 fusion.26
  111.7 0.4 convolution_add_fusion
  112.3 0.2 reshape.141
  112.5 2.0 %copy.50 = f32[16,1,8,520]{0,2,3,1:T(8,128)} copy(f32[16,1,8,520]{3,2,0,1:T(8,128)S(1)} %reshape.141) | data formatting | bytes 532480 | tf_op jit(solution)/shard_map/conv_general_dilated | solution.py:31
  114.5 1.0 slice.152
  115.5 12.7 %fusion.11 = bf16[8,520,16]{2,0,1:T(8,128)(2,1)} fusion(f32[16,1,64]{0,1,2:T(1,128)S(1)} %bitcast.169, f32[16,1,7,63]{0,2,3,1:T(8,128)S(1)} %slice.152, f32[16,1,8,520]{0,2,3,1:T(8,128)} %copy.50), kind=kOutput, calls=%fused_computation.17 | convolution fusion | flops 51341952 | bytes 431680 | tf_op jit(solution)/shard_map/conv_general_dilated | solution.py:31
  128.2 1.8 copy.52
  130.2 0.2 reshape.145
  130.3 0.1 convert_reduce_fusion.2
  130.5 0.2 fusion.20
  130.8 0.4 fusion.23
  131.2 0.1 reshape.136
  131.4 0.8 fusion.31
  132.2 3.3 %all-to-all-start.1 = ((bf16[4,16,1024]{2,1,0:T(8,128)(2,1)}), bf16[4,16,1024]{2,1,0:T(8,128)(2,1)S(1)}, u32[]{:S(2)}, u32[]{:S(2)}) async-start(bf16[4,16,1024]{2,1,0:T(8,128)(2,1)} %fusion.31), calls=%async_computation.1 | async-start | bytes 262144 | tf_op jit(solution)/shard_map/all_to_all | solution.py:99
  135.5 2.4 %fusion.1 = f32[2048]{0:T(1024)S(1)} fusion(f32[2048]{0:T(1024)S(1)} %broadcast_multiply_fusion, bf16[512,2048]{1,0:T(8,128)(2,1)S(1)} %fusion.7, bf16[512,2048]{1,0:T(8,128)(2,1)} %fusion.6), kind=kLoop, calls=%fused_computation.3 | loop fusion | flops 14678016 | bytes 4210688 | tf_op jit(solution)/shard_map/reduce_sum | solution.py:51
  138.0 0.6 pad_maximum_fusion.5
  138.6 2.8 %all-to-all-done.1 = bf16[4,16,1024]{2,1,0:T(8,128)(2,1)S(1)} async-done(((bf16[4,16,1024]{2,1,0:T(8,128)(2,1)}), bf16[4,16,1024]{2,1,0:T(8,128)(2,1)S(1)}, u32[]{:S(2)}, u32[]{:S(2)}) %all-to-all-start.1) | async-done | bytes 131104 | tf_op jit(solution)/shard_map/all_to_all | solution.py:99
  141.4 3.2 %all-to-all-start.3 = ((f32[2,4,512]{2,0,1:T(2,128)}), f32[2,4,512]{2,0,1:T(2,128)S(1)}, u32[]{:S(2)}, u32[]{:S(2)}) async-start(f32[2,4,512]{2,0,1:T(2,128)} %pad_maximum_fusion.5), calls=%async_computation.3 | async-start | bytes 32768 | tf_op jit(solution)/shard_map/all_to_all | solution.py:110
  144.7 7.0 %all_gather.7 = bf16[4,64,1024]{2,1,0:T(8,128)(2,1)S(1)} all-gather(bf16[4,16,1024]{2,1,0:T(8,128)(2,1)S(1)} %all-to-all-done.1), channel_id=1, replica_groups=mesh['wind'=2,'gx'=4,'gy'=2,'gz'=2] {'gy','gz'}, dimensions={1}, use_global_device_ids=true | all-gather | bytes 655360 | tf_op jit(solution)/shard_map/all_gather | solution.py:100
  151.7 3.5 %convolution_convert_fusion = bf16[256,2048]{1,0:T(8,128)(2,1)S(1)} fusion(bf16[256,1024]{1,0:T(8,128)(2,1)S(1)} %bitcast.166, bf16[1024,2048]{1,0:T(8,128)(2,1)} %param.5), kind=kOutput, calls=%fused_computation.14 | convolution fusion | flops 1074266112 | bytes 5767168 | tf_op jit(solution)/shard_map/dot_general | solution.py:12
  155.1 1.1 copy.88
  156.2 5.0 %all-to-all-start.2 = ((bf16[256,4,512]{2,0,1:T(8,128)(2,1)}), bf16[256,4,512]{2,0,1:T(8,128)(2,1)S(1)}, u32[]{:S(2)}, u32[]{:S(2)}) async-start(bf16[256,4,512]{2,0,1:T(8,128)(2,1)} %bitcast.160), calls=%async_computation.2 | async-start | bytes 2097152 | tf_op jit(solution)/shard_map/all_to_all | solution.py:102
  161.3 26.2 %all-to-all-done.2 = bf16[256,4,512]{2,0,1:T(8,128)(2,1)S(1)} async-done(((bf16[256,4,512]{2,0,1:T(8,128)(2,1)}), bf16[256,4,512]{2,0,1:T(8,128)(2,1)S(1)}, u32[]{:S(2)}, u32[]{:S(2)}) %all-to-all-start.2) | async-done | bytes 1048608 | tf_op jit(solution)/shard_map/all_to_all | solution.py:102
  187.5 0.1 convert_reduce_fusion.1
  187.6 1.2 reshape_divide_fusion
  (66 shorter events, 1.1 us)
Async XLA Ops:
  7.2 13.4 %copy-start.4 = (s32[256]{0:T(256)S(1)}, s32[256]{0:T(256)}, u32[]{:S(2)}) copy-start(s32[256]{0:T(256)} %param.9) | copy-start | bytes 3076
  7.2 13.5 %copy-start.2 = (f32[256,64]{0,1:T(8,128)S(1)}, f32[256,64]{0,1:T(8,128)}, u32[]{:S(2)}) copy-start(f32[256,64]{0,1:T(8,128)} %param.8) | copy-start | bytes 196612
  7.2 46.8 %all-gather.3.cloned.1.call-start = ((), (), s32[]{:S(2)}) async-start(), calls=%async_computation.4 | async-start | bytes 1310720 | tf_op jit(solution)/shard_map/all_gather | solution.py:64
  7.9 88.3 %all-reduce.7.cloned.1.call-start = ((), (), s32[]{:S(2)}) async-start(), calls=%async_computation.5 | async-start | bytes 2097152
  10.3 51.2 %collective-permute-start = (bf16[256,2048]{1,0:T(8,128)(2,1)}, bf16[256,2048]{1,0:T(8,128)(2,1)}, u32[]{:S(2)}, u32[]{:S(2)}) collective-permute-start(bf16[256,2048]{1,0:T(8,128)(2,1)} %slice.128), channel_id=1, source_target_pairs={{0,4},{4,8},{8,12},{1,5},{5,9},{9,13},{2,6},{6,10},{10,14},{3,7},{... | collective-permute-start | bytes 3145736 | tf_op jit(solution)/shard_map/ppermute | solution.py:65
  27.5 32.7 %copy-start.5 = (u32[32]{0:T(128)S(1)}, u32[32]{0:T(128)}, u32[]{:S(2)}) copy-start(u32[32]{0:T(128)} %constant.69) | copy-start | bytes 388
  98.0 13.0 %all-to-all-start = ((f32[4,16,1024]{2,1,0:T(8,128)}), f32[4,16,1024]{2,1,0:T(8,128)S(1)}, u32[]{:S(2)}, u32[]{:S(2)}) async-start(f32[4,16,1024]{2,1,0:T(8,128)} %copy.45), calls=%async_computation | async-start | bytes 524288 | tf_op jit(solution)/shard_map/all_to_all | solution.py:70
  115.5 14.6 %copy-start.3 = (pred[8,520]{1,0:T(8,128)(4,1)S(1)}, pred[8,520]{1,0:T(8,128)(4,1)}, u32[]{:S(2)}) copy-start(pred[8,520]{1,0:T(8,128)(4,1)} %constant.66) | copy-start | bytes 12484
  115.5 15.3 %copy-start = (bf16[512,768]{1,0:T(8,128)(2,1)S(1)}, bf16[512,768]{1,0:T(8,128)(2,1)}, u32[]{:S(2)}) copy-start(bf16[512,768]{1,0:T(8,128)(2,1)} %reshape.135) | copy-start | bytes 2359300
  130.5 24.6 %copy-start.1 = (bf16[16,4096]{1,0:T(8,128)(2,1)}, bf16[16,4096]{1,0:T(8,128)(2,1)S(1)}, u32[]{:S(2)}) copy-start(bf16[16,4096]{1,0:T(8,128)(2,1)S(1)} %get-tuple-element.3) | copy-start | bytes 393220
  132.2 9.2 %all-to-all-start.1 = ((bf16[4,16,1024]{2,1,0:T(8,128)(2,1)}), bf16[4,16,1024]{2,1,0:T(8,128)(2,1)S(1)}, u32[]{:S(2)}, u32[]{:S(2)}) async-start(bf16[4,16,1024]{2,1,0:T(8,128)(2,1)} %fusion.31), calls=%async_computation.1 | async-start | bytes 262144 | tf_op jit(solution)/shard_map/all_to_all | solution.py:99
  141.4 14.8 %all-to-all-start.3 = ((f32[2,4,512]{2,0,1:T(2,128)}), f32[2,4,512]{2,0,1:T(2,128)S(1)}, u32[]{:S(2)}, u32[]{:S(2)}) async-start(f32[2,4,512]{2,0,1:T(2,128)} %pad_maximum_fusion.5), calls=%async_computation.3 | async-start | bytes 32768 | tf_op jit(solution)/shard_map/all_to_all | solution.py:110
  156.2 31.3 %all-to-all-start.2 = ((bf16[256,4,512]{2,0,1:T(8,128)(2,1)}), bf16[256,4,512]{2,0,1:T(8,128)(2,1)S(1)}, u32[]{:S(2)}, u32[]{:S(2)}) async-start(bf16[256,4,512]{2,0,1:T(8,128)(2,1)} %bitcast.160), calls=%async_computation.2 | async-start | bytes 2097152 | tf_op jit(solution)/shard_map/all_to_all | solution.py:102
Sparse Core Ops, SparseCore 0:
  9.6 44.3 all-gather.2
  59.6 36.5 all-reduce.6
where the time goes:
time: 196 us
  waiting for transfers between devices  92 us (47%)
  matrix products  29.8 us (15%)
  starting transfers between devices  22.2 us (11%)
  local copies, waits for them, and re-layouts  20 us (10%)
  between operations  15.2 us (8%)
  other arithmetic  9.45 us (5%)
  blocking collectives  6.99 us (4%)
    unnamed x3, waiting for transfers between devices  30.4 us
    all_gather x1, waiting for transfers between devices, body(): lax.all_gather(influence.reshape(modes, -1), 'gx', axis=1, tiled=True)  26.4 us
    all_to_all x1, waiting for transfers between devices, body(): lax.all_to_all(cross.reshape(modes, nx, own_panels), 'gx', split_axis=1,...  26.2 us
    dot_general x7, matrix products, dot(): lax.dot_general(a, b, (contract, ((), ())), preferred_element_type=F32)  17.1 us
    conv_general_dilated x1, matrix products, dynamic_filter(): lax.conv_general_dilated(series[None], kernel_taps[:, None, :], window_st...  12.7 us
    all_gather x1, blocking collectives, body(): lax.all_gather(back, ('gy', 'gz'), axis=1, tiled=True).reshape(modes, rows)  6.99 us
    all_to_all x1, waiting for transfers between devices, body(): raw = lax.all_to_all(raw, 'gx', split_axis=0, concat_axis=0, tiled=True)  6.18 us
    ppermute x1, starting transfers between devices, body(): lax.ppermute(pressure[rows - rim:], 'gx', [(i, i + 1) for i in range(nx -...  5.89 us
  transfers between devices with their start and end apart: 7, of which 5 were waited for; matrix products, arithmetic and copies ran while one was open for 18% of the time, Pallas kernels for 0%

commit v1 on v0

--- a/solution.py
+++ b/solution.py
@@ -6,6 +6,28 @@
 
 F32 = jnp.float32
 BF16 = jnp.bfloat16
+
+
+def laid_out(parts, dim):
+    dims = list(parts.shape[1:])
+    dims[dim] *= parts.shape[0]
+    return jnp.moveaxis(parts, 0, dim).reshape(dims)
+
+
+def gather_around(value, axis, dim):
+    peers = lax.axis_size(axis)
+    pairs = [(i, (i + 1) % peers) for i in range(peers)]
+    back = [(b, a) for a, b in pairs]
+    lower, upper = ([], [])
+    for turn in range(peers - 1):
+        if turn % 2 == 0:
+            lower.append(lax.ppermute(lower[-1] if lower else value, axis, pairs))
+        else:
+            upper.append(lax.ppermute(upper[-1] if upper else value, axis, back))
+    pieces = jnp.stack([*lower[::-1], value, *upper])
+    shift = lax.axis_index(axis) - len(lower)
+    pieces = pieces[(jnp.arange(peers) - shift) % peers]
+    return laid_out(pieces, dim)
 
 
 def dot(a, b, contract):
@@ -97,7 +119,7 @@
     back = ((back - mean_mode[:, None] * reach[None, :]) * scale[:, None]).astype(BF16)
     back = back.reshape(own, nx, rows).transpose(1, 0, 2)
     back = lax.all_to_all(back, "gx", split_axis=0, concat_axis=0, tiled=True)
-    back = lax.all_gather(back, ("gy", "gz"), axis=1, tiled=True).reshape(modes, rows)
+    back = gather_around(back, ("gy", "gz"), 1).reshape(modes, rows)
     cross = dot(back, pressure, ((1,), (0,))).astype(BF16)
     cross = lax.all_to_all(
         cross.reshape(modes, nx, own_panels), "gx", split_axis=1, concat_axis=1, tiled=True

time: 196 us -> 198 us (1.010)
  blocking collectives: 6.99 us -> 0 us
  waiting for transfers between devices: 92 us -> 98.6 us
    all_gather x1 -> x0, blocking collectives: 6.99 us -> none  [body(): lax.all_gather(back, ('gy', 'gz'), axis=1, tiled=True).reshape(modes, rows)]
    unnamed x3, waiting for transfers between devices: 30.4 us -> 33.7 us
    all_to_all x1, waiting for transfers between devices: 6.18 us -> 3.44 us  [body(): raw = lax.all_to_all(raw, 'gx', split_axis=0, concat_axis=0, tiled=True)]
    ppermute x0 -> x3, waiting for transfers between devices: none -> 2.65 us  [the longest x2 2.65 us: gather_around(): lower.append(lax.ppermute(lower[-1] if lower else value, axis, pairs))]
  transfers between devices with their start and end apart: 7 -> 10, of which waited for: 5 -> 7; matrix products, arithmetic and copies ran while one was open for 18% -> 19% of each run, Pallas kernels for 0% -> 0%
where the time goes in v1:
time: 198 us; the launch traced here: 197 us
  waiting for transfers between devices  98.6 us (50%)
  matrix products  29.7 us (15%)
  starting transfers between devices  23.6 us (12%)
  local copies, waits for them, and re-layouts  20.7 us (10%)
  between operations  15.3 us (8%)
  other arithmetic  9.54 us (5%)
    unnamed x3, waiting for transfers between devices  33.7 us
    all_gather x1, waiting for transfers between devices, body(): lax.all_gather(influence.reshape(modes, -1), 'gx', axis=1, tiled=True)  28 us
    all_to_all x1, waiting for transfers between devices, body(): lax.all_to_all(cross.reshape(modes, nx, own_panels), 'gx', split_axis=1,...  26.8 us
    dot_general x7, matrix products, dot(): lax.dot_general(a, b, (contract, ((), ())), preferred_element_type=F32)  17.1 us
    conv_general_dilated x1, matrix products, dynamic_filter(): lax.conv_general_dilated(series[None], kernel_taps[:, None, :], window_st...  12.7 us
    ppermute x1, starting transfers between devices, body(): lax.ppermute(pressure[rows - rim:], 'gx', [(i, i + 1) for i in range(nx -...  5.91 us
    conv_general_dilated x4, local copies, waits for them, and re-layouts, dynamic_filter(): lax.conv_general_dilated(series[None], kernel_taps[:, None, :], window_st...  5.04 us
    all_to_all x1, starting transfers between devices, body(): lax.all_to_all(cross.reshape(modes, nx, own_panels), 'gx', split_axis=1,...  4.71 us
  transfers between devices with their start and end apart: 10, of which 7 were waited for; matrix products, arithmetic and copies ran while one was open for 19% of the time, Pallas kernels for 0%

profile of v1, /device:TPU:0, one launch (start us, length us, event | category | flops | bytes accessed | tf_op | source)
XLA Modules:
  0.0 197.4 jit_solution(11541565003707102893)
XLA Ops:
  7.2 0.7 all-gather.3.cloned.1.call-update
  8.0 2.4 %slice.128 = bf16[256,2048]{1,0:T(8,128)(2,1)} slice(bf16[1024,2048]{1,0:T(8,128)(2,1)} %param.5), slice={[768:1024], [0:2048]} | slice | bytes 2097152 | tf_op jit(solution)/shard_map/slice | solution.py:87
  10.3 5.9 %collective-permute-start.3 = (bf16[256,2048]{1,0:T(8,128)(2,1)}, bf16[256,2048]{1,0:T(8,128)(2,1)}, u32[]{:S(2)}, u32[]{:S(2)}) collective-permute-start(bf16[256,2048]{1,0:T(8,128)(2,1)} %slice.128), channel_id=1, source_target_pairs={{0,4},{4,8},{8,12},{1,5},{5,9},{9,13},{2,6},{6,10},{10,14},{3,7},{... | collective-permute-start | bytes 3145736 | tf_op jit(solution)/shard_map/ppermute | solution.py:87
  16.3 0.7 convert_element_type.45
  16.9 0.8 reverse
  17.8 0.7 concatenate.16
  18.5 1.3 tile.9
  20.0 0.7 reshape.178
  20.9 1.3 tile.11
  22.3 1.6 reshape.181
  23.9 0.8 select_reduce_fusion
  24.7 0.6 dynamic-slice
  26.0 28.0 %all-gather.3.cloned.1.call-done = bf16[256,1,1,2048]{3,0,2,1:T(8,128)(2,1)} async-done(((bf16[256,1,1,512]{3,0,2,1:T(8,128)(2,1)}), bf16[256,1,1,2048]{3,0,2,1:T(8,128)(2,1)}) %all-gather.3.cloned.1.call-update) | async-done | bytes 1048592 | tf_op jit(solution)/shard_map/all_gather | solution.py:86
  54.0 3.8 %fusion.17 = f32[256,1024]{1,0:T(8,128)S(1)} fusion(bf16[1024,2048]{1,0:T(8,128)(2,1)} %param.5, bf16[256,1,1,2048]{3,0,2,1:T(8,128)(2,1)} %all-gather.3.cloned.1.call-done), kind=kOutput, calls=%fused_computation.27 | convolution fusion | flops 1073741824 | bytes 6291456 | tf_op jit(solution)/shard_map/dot_general | solution.py:34
  57.8 1.7 copy.55
  59.5 3.7 %fusion.7 = bf16[512,2048]{1,0:T(8,128)(2,1)S(1)} fusion(bf16[512,768]{1,0:T(8,128)(2,1)S(1)} %reshape.178, bf16[1024,2048]{1,0:T(8,128)(2,1)} %param.5), kind=kOutput, calls=%fused_computation.14 | convolution fusion | flops 1611661312 | bytes 6029312 | tf_op jit(solution)/shard_map/dot_general | solution.py:34
  63.2 33.0 %all-reduce.7.cloned.1.call-done = f32[4,64,1024]{2,0,1:T(4,128)} async-done(((f32[4,64,1024]{2,0,1:T(4,128)}), f32[4,64,1024]{2,0,1:T(4,128)}) %all-reduce.7.cloned.1.call-update) | async-done | bytes 1048592
  96.2 1.0 constant_dynamic-slice_fusion
  97.2 0.9 copy.56
  98.0 4.6 %all-to-all-start = ((f32[4,16,1024]{2,1,0:T(8,128)}), f32[4,16,1024]{2,1,0:T(8,128)S(1)}, u32[]{:S(2)}, u32[]{:S(2)}) async-start(f32[4,16,1024]{2,1,0:T(8,128)} %copy.56), calls=%async_computation | async-start | bytes 524288 | tf_op jit(solution)/shard_map/all_to_all | solution.py:92
  102.6 5.0 %fusion.6 = bf16[512,2048]{1,0:T(8,128)(2,1)} fusion(bf16[512,768]{1,0:T(8,128)(2,1)S(1)} %reshape.178, bf16[1024,2048]{1,0:T(8,128)(2,1)} %param.5, bf16[256,2048]{1,0:T(8,128)(2,1)} %collective-permute-done.3), kind=kOutput, calls=%fused_computation.13 | convolution fusion | flops 1617952768 | bytes 8126464 | tf_op jit(solution)/shard_map/dot_general | solution.py:34
  107.6 3.4 %all-to-all-done = f32[4,16,1024]{2,1,0:T(8,128)S(1)} async-done(((f32[4,16,1024]{2,1,0:T(8,128)}), f32[4,16,1024]{2,1,0:T(8,128)S(1)}, u32[]{:S(2)}, u32[]{:S(2)}) %all-to-all-start) | async-done | bytes 262176 | tf_op jit(solution)/shard_map/all_to_all | solution.py:92
  111.2 0.4 fusion.26
  111.7 0.4 convolution_add_fusion
  112.3 0.2 reshape.186
  112.5 2.0 %copy.61 = f32[16,1,8,520]{0,2,3,1:T(8,128)} copy(f32[16,1,8,520]{3,2,0,1:T(8,128)S(1)} %reshape.186) | data formatting | bytes 532480 | tf_op jit(solution)/shard_map/conv_general_dilated | solution.py:53
  114.5 1.0 slice.154
  115.5 12.7 %fusion.11 = bf16[8,520,16]{2,0,1:T(8,128)(2,1)} fusion(f32[16,1,64]{0,1,2:T(1,128)S(1)} %bitcast.181, f32[16,1,7,63]{0,2,3,1:T(8,128)S(1)} %slice.154, f32[16,1,8,520]{0,2,3,1:T(8,128)} %copy.61), kind=kOutput, calls=%fused_computation.18 | convolution fusion | flops 51341952 | bytes 431680 | tf_op jit(solution)/shard_map/conv_general_dilated | solution.py:53
  128.2 1.8 copy.63
  130.1 0.2 reshape.190
  130.5 0.2 fusion.20
  130.8 0.4 fusion.23
  131.3 0.8 fusion.31
  132.2 3.3 %all-to-all-start.1 = ((bf16[4,16,1024]{2,1,0:T(8,128)(2,1)}), bf16[4,16,1024]{2,1,0:T(8,128)(2,1)S(1)}, u32[]{:S(2)}, u32[]{:S(2)}) async-start(bf16[4,16,1024]{2,1,0:T(8,128)(2,1)} %fusion.31), calls=%async_computation.1 | async-start | bytes 262144 | tf_op jit(solution)/shard_map/all_to_all | solution.py:121
  135.5 2.2 %convert_reduce_fusion = f32[2048]{0:T(1024)S(1)} fusion(bf16[512,2048]{1,0:T(8,128)(2,1)S(1)} %fusion.7, bf16[512,2048]{1,0:T(8,128)(2,1)} %fusion.6), kind=kLoop, calls=%fused_computation.2 | loop fusion | flops 10483712 | bytes 4202496 | tf_op jit(solution)/shard_map/reduce_sum | solution.py:72
  137.7 3.7 %all-to-all-done.1 = bf16[4,16,1024]{2,1,0:T(8,128)(2,1)S(1)} async-done(((bf16[4,16,1024]{2,1,0:T(8,128)(2,1)}), bf16[4,16,1024]{2,1,0:T(8,128)(2,1)S(1)}, u32[]{:S(2)}, u32[]{:S(2)}) %all-to-all-start.1) | async-done | bytes 131104 | tf_op jit(solution)/shard_map/all_to_all | solution.py:121
  141.4 1.7 collective-permute-start.2
  143.1 2.6 %collective-permute-done = bf16[4,16,1024]{2,1,0:T(8,128)(2,1)S(1)} collective-permute-done((bf16[4,16,1024]{2,1,0:T(8,128)(2,1)S(1)}, bf16[4,16,1024]{2,1,0:T(8,128)(2,1)S(1)}, u32[]{:S(2)}, u32[]{:S(2)}) %collective-permute-start) | collective-permute-done | bytes 131104 | tf_op jit(solution)/shard_map/ppermute | solution.py:24
  145.8 2.4 %fusion.1 = f32[2048]{0:T(1024)S(1)} fusion(f32[2048]{0:T(1024)S(1)} %broadcast_multiply_fusion, bf16[512,2048]{1,0:T(8,128)(2,1)S(1)} %fusion.7, bf16[512,2048]{1,0:T(8,128)(2,1)} %fusion.6), kind=kLoop, calls=%fused_computation.4 | loop fusion | flops 14678016 | bytes 4210688 | tf_op jit(solution)/shard_map/reduce_sum | solution.py:73
  148.2 0.6 pad_maximum_fusion.6
  148.8 3.3 %all-to-all-start.3 = ((f32[2,4,512]{2,0,1:T(2,128)}), f32[2,4,512]{2,0,1:T(2,128)S(1)}, u32[]{:S(2)}, u32[]{:S(2)}) async-start(f32[2,4,512]{2,0,1:T(2,128)} %pad_maximum_fusion.6), calls=%async_computation.3 | async-start | bytes 32768 | tf_op jit(solution)/shard_map/all_to_all | solution.py:132
  152.2 0.6 gather_fusion
  152.8 3.5 %convolution_convert_fusion = bf16[256,2048]{1,0:T(8,128)(2,1)S(1)} fusion(bf16[256,1024]{1,0:T(8,128)(2,1)S(1)} %bitcast.174, bf16[1024,2048]{1,0:T(8,128)(2,1)} %param.5), kind=kOutput, calls=%fused_computation.15 | convolution fusion | flops 1074266112 | bytes 5767168 | tf_op jit(solution)/shard_map/dot_general | solution.py:34
  156.3 1.1 copy.100
  157.4 0.3 all-to-all-done.3
  157.7 4.7 %all-to-all-start.2 = ((bf16[256,4,512]{2,0,1:T(8,128)(2,1)}), bf16[256,4,512]{2,0,1:T(8,128)(2,1)S(1)}, u32[]{:S(2)}, u32[]{:S(2)}) async-start(bf16[256,4,512]{2,0,1:T(8,128)(2,1)} %bitcast.167), calls=%async_computation.2 | async-start | bytes 2097152 | tf_op jit(solution)/shard_map/all_to_all | solution.py:124
  162.5 26.8 %all-to-all-done.2 = bf16[256,4,512]{2,0,1:T(8,128)(2,1)S(1)} async-done(((bf16[256,4,512]{2,0,1:T(8,128)(2,1)}), bf16[256,4,512]{2,0,1:T(8,128)(2,1)S(1)}, u32[]{:S(2)}, u32[]{:S(2)}) %all-to-all-start.2) | async-done | bytes 1048608 | tf_op jit(solution)/shard_map/all_to_all | solution.py:124
  189.4 1.2 reshape_divide_fusion
  (76 shorter events, 1.7 us)
Async XLA Ops:
  7.2 13.5 %copy-start.4 = (s32[256]{0:T(256)S(1)}, s32[256]{0:T(256)}, u32[]{:S(2)}) copy-start(s32[256]{0:T(256)} %param.9) | copy-start | bytes 3076
  7.2 13.6 %copy-start.2 = (f32[256,64]{0,1:T(8,128)S(1)}, f32[256,64]{0,1:T(8,128)}, u32[]{:S(2)}) copy-start(f32[256,64]{0,1:T(8,128)} %param.8) | copy-start | bytes 196612
  7.2 46.8 %all-gather.3.cloned.1.call-start = ((), (), s32[]{:S(2)}) async-start(), calls=%async_computation.4 | async-start | bytes 1310720 | tf_op jit(solution)/shard_map/all_gather | solution.py:86
  7.9 88.3 %all-reduce.7.cloned.1.call-start = ((), (), s32[]{:S(2)}) async-start(), calls=%async_computation.5 | async-start | bytes 2097152
  10.3 92.3 %collective-permute-start.3 = (bf16[256,2048]{1,0:T(8,128)(2,1)}, bf16[256,2048]{1,0:T(8,128)(2,1)}, u32[]{:S(2)}, u32[]{:S(2)}) collective-permute-start(bf16[256,2048]{1,0:T(8,128)(2,1)} %slice.128), channel_id=1, source_target_pairs={{0,4},{4,8},{8,12},{1,5},{5,9},{9,13},{2,6},{6,10},{10,14},{3,7},{... | collective-permute-start | bytes 3145736 | tf_op jit(solution)/shard_map/ppermute | solution.py:87
  20.0 4.8 %copy-start.5 = (u32[32]{0:T(128)S(1)}, u32[32]{0:T(128)}, u32[]{:S(2)}) copy-start(u32[32]{0:T(128)} %constant.85) | copy-start | bytes 388
  98.0 13.0 %all-to-all-start = ((f32[4,16,1024]{2,1,0:T(8,128)}), f32[4,16,1024]{2,1,0:T(8,128)S(1)}, u32[]{:S(2)}, u32[]{:S(2)}) async-start(f32[4,16,1024]{2,1,0:T(8,128)} %copy.56), calls=%async_computation | async-start | bytes 524288 | tf_op jit(solution)/shard_map/all_to_all | solution.py:92
  115.5 14.5 %copy-start.3 = (pred[8,520]{1,0:T(8,128)(4,1)S(1)}, pred[8,520]{1,0:T(8,128)(4,1)}, u32[]{:S(2)}) copy-start(pred[8,520]{1,0:T(8,128)(4,1)} %constant.82) | copy-start | bytes 12484
  115.5 15.3 %copy-start = (bf16[512,768]{1,0:T(8,128)(2,1)S(1)}, bf16[512,768]{1,0:T(8,128)(2,1)}, u32[]{:S(2)}) copy-start(bf16[512,768]{1,0:T(8,128)(2,1)} %reshape.181) | copy-start | bytes 2359300
  130.4 17.8 %copy-start.1 = (bf16[16,4096]{1,0:T(8,128)(2,1)}, bf16[16,4096]{1,0:T(8,128)(2,1)S(1)}, u32[]{:S(2)}) copy-start(bf16[16,4096]{1,0:T(8,128)(2,1)S(1)} %get-tuple-element.3) | copy-start | bytes 393220
  132.2 9.2 %all-to-all-start.1 = ((bf16[4,16,1024]{2,1,0:T(8,128)(2,1)}), bf16[4,16,1024]{2,1,0:T(8,128)(2,1)S(1)}, u32[]{:S(2)}, u32[]{:S(2)}) async-start(bf16[4,16,1024]{2,1,0:T(8,128)(2,1)} %fusion.31), calls=%async_computation.1 | async-start | bytes 262144 | tf_op jit(solution)/shard_map/all_to_all | solution.py:121
  141.4 4.4 %collective-permute-start = (bf16[4,16,1024]{2,1,0:T(8,128)(2,1)S(1)}, bf16[4,16,1024]{2,1,0:T(8,128)(2,1)S(1)}, u32[]{:S(2)}, u32[]{:S(2)}) collective-permute-start(bf16[4,16,1024]{2,1,0:T(8,128)(2,1)S(1)} %all-to-all-done.1), channel_id=1, source_target_pairs={{0,1},{1,2},{2,3},{3,0},{4,5},{5,6},{6,7},{7,4},{8,9},{9,10},{10,1... | collective-permute-start | bytes 393224 | tf_op jit(solution)/shard_map/ppermute | solution.py:24
  141.4 10.7 %collective-permute-start.2 = (bf16[4,16,1024]{2,1,0:T(8,128)(2,1)S(1)}, bf16[4,16,1024]{2,1,0:T(8,128)(2,1)S(1)}, u32[]{:S(2)}, u32[]{:S(2)}) collective-permute-start(bf16[4,16,1024]{2,1,0:T(8,128)(2,1)S(1)} %all-to-all-done.1), channel_id=1, source_target_pairs={{1,0},{2,1},{3,2},{0,3},{5,4},{6,5},{7,6},{4,7},{9,8},{10,9},{11,1... | collective-permute-start | bytes 393224 | tf_op jit(solution)/shard_map/ppermute | solution.py:26
  145.8 6.3 %collective-permute-start.1 = (bf16[4,16,1024]{2,1,0:T(8,128)(2,1)S(1)}, bf16[4,16,1024]{2,1,0:T(8,128)(2,1)S(1)}, u32[]{:S(2)}, u32[]{:S(2)}) collective-permute-start(bf16[4,16,1024]{2,1,0:T(8,128)(2,1)S(1)} %collective-permute-done), channel_id=1, source_target_pairs={{0,1},{1,2},{2,3},{3,0},{4,5},{5,6},{6,7},{7,4},{8,9},{9,10},{10,1... | collective-permute-start | bytes 393224 | tf_op jit(solution)/shard_map/ppermute | solution.py:24
  148.8 8.9 %all-to-all-start.3 = ((f32[2,4,512]{2,0,1:T(2,128)}), f32[2,4,512]{2,0,1:T(2,128)S(1)}, u32[]{:S(2)}, u32[]{:S(2)}) async-start(f32[2,4,512]{2,0,1:T(2,128)} %pad_maximum_fusion.6), calls=%async_computation.3 | async-start | bytes 32768 | tf_op jit(solution)/shard_map/all_to_all | solution.py:132
  157.7 31.6 %all-to-all-start.2 = ((bf16[256,4,512]{2,0,1:T(8,128)(2,1)}), bf16[256,4,512]{2,0,1:T(8,128)(2,1)S(1)}, u32[]{:S(2)}, u32[]{:S(2)}) async-start(bf16[256,4,512]{2,0,1:T(8,128)(2,1)} %bitcast.167), calls=%async_computation.2 | async-start | bytes 2097152 | tf_op jit(solution)/shard_map/all_to_all | solution.py:124
Sparse Core Ops, SparseCore 0:
  9.6 44.3 all-gather.2
  59.6 36.5 all-reduce.6
